TPU v7x, 32 devices: a whole 2x2x4 slice. The times are simulated.
32 devices in a mesh: shot: 4 (over y, core), dom: 8 (over z, x).
Axes of the slice: x: 2, y: 2, z: 4, core: 2. Of those that a mesh axis runs over, the one named last changes fastest.
Arguments:
- model_slab: float32 [128, 128, 128], P('dom'), may hold values from 0.0225 to 0.17
- wave_prev: float32 [4, 128, 128, 128], P('shot', 'dom'), may hold values from -6 to 6
- wave_now: float32 [4, 128, 128, 128], P('shot', 'dom'), may hold values from -6 to 6
- adjoint_next: float32 [4, 128, 128, 128], P('shot', 'dom'), may hold values from -6 to 6
- adjoint_now: float32 [4, 128, 128, 128], P('shot', 'dom'), may hold values from -6 to 6
- wavelet: float32 [4, 8], P('shot'), may hold values from -12 to 12
- source_cell: int32 [4], P('shot'), may hold values from 0 to 2097151
- receiver_cells: int32 [4, 256], P('shot'), may hold values from 0 to 2097151
- observed: float32 [4, 8, 256], P('shot'), may hold values from -6 to 6
Outputs:
- direction: float32 [128, 128, 128], P('dom')
- new_model: float32 [128, 128, 128], P('dom')
Inputs may be any that keep to these rules, and one draw needn't show every extreme that they name: `source_cell`: flat cell index x * 128 * 128 + y * 128 + z. `receiver_cells`: flat cell indices x * 128 * 128 + y * 128 + z; a cell may repeat.
All inputs are finite; a program needn't handle non-finite values. Where the computation divides by a largest or mean magnitude, that divisor is 1e-20 or more.
Results may differ from a plain program's by a relative error of at most 0.000025.
Values sent between devices are 32-bit elements; how exact they have to be, the bound alone decides.
A program may use at most 192 MiB of HBM per device.

v0:
```python
import jax
import jax.numpy as jnp
from jax import lax
from jax.sharding import PartitionSpec as P

STEPS = 8


COEFFS = (8.0 / 5.0, -1.0 / 5.0, 8.0 / 315.0, -1.0 / 560.0)
CENTRE = -205.0 / 72.0
STEP_FRACTION = 0.1
EPSILON = 1e-06


def padded_2(cells, sides, width):
    for axis, dim in sides:
        count = lax.axis_size(axis)
        ends = count - 1
        head = lax.slice_in_dim(cells, 0, width, axis=dim)
        tail = lax.slice_in_dim(cells, cells.shape[dim] - width, cells.shape[dim], axis=dim)
        cells = jnp.concatenate(
            [
                lax.ppermute(tail, axis, [(i, (i + 1) % count) for i in range(ends)]),
                cells,
                lax.ppermute(head, axis, [((i + 1) % count, i) for i in range(ends)]),
            ],
            axis=dim,
        )
    return cells


def shifted(field, axis, offset):
    length = field.shape[axis]
    filler_shape = list(field.shape)
    filler_shape[axis] = abs(offset)
    filler = jnp.zeros(filler_shape, field.dtype)
    if offset > 0:
        return jnp.concatenate([lax.slice_in_dim(field, offset, length, axis=axis), filler], axis)
    return jnp.concatenate([filler, lax.slice_in_dim(field, 0, length + offset, axis=axis)], axis)


def laplace(padded):
    rows = padded.shape[0] - 8
    field = padded[4 : 4 + rows]
    total = 3.0 * CENTRE * field
    for index, weight in enumerate(COEFFS):
        offset = index + 1
        total = total + weight * (
            padded[4 + offset : 4 + offset + rows] + padded[4 - offset : 4 - offset + rows]
        )
    for axis in (1, 2):
        for index, weight in enumerate(COEFFS):
            offset = index + 1
            total = total + weight * (shifted(field, axis, offset) + shifted(field, axis, -offset))
    return total


def add_at(field, start_row, targets, amounts):
    count = field.size
    plane = field.shape[1] * field.shape[2]
    relative = targets - start_row * plane
    inside = (relative >= 0) & (relative < count)
    slots = jnp.clip(relative, 0, count - 1)
    values = jnp.where(inside, amounts, 0.0)
    return field.reshape(-1).at[slots].add(values).reshape(field.shape)


def on_device(
    model_slab,
    wave_prev,
    wave_now,
    adjoint_next,
    adjoint_now,
    wavelet,
    source_cell,
    receiver_cells,
    observed,
):
    shape = model_slab.shape
    rows = shape[0]
    cells = shape[0] * shape[1] * shape[2]
    own_row = lax.axis_index("dom") * rows
    first_cell = own_row * shape[1] * shape[2]
    source_one = source_cell[0]
    receivers = receiver_cells[0]
    receiver_local = receivers - first_cell
    receiver_inside = (receiver_local >= 0) & (receiver_local < cells)
    receiver_slots = jnp.clip(receiver_local, 0, cells - 1)
    images = []
    residuals = []
    gradient = jnp.zeros(shape, jnp.float32)
    older, current = (wave_prev[0], wave_now[0])
    for tick in range(STEPS):
        padded = padded_2(current, (("dom", 0),), 4)
        image = laplace(padded)
        newer = 2.0 * current - older + model_slab * image
        newer = add_at(newer, own_row, source_one, wavelet[0, tick])
        values = newer.reshape(-1)[receiver_slots] - observed[0, tick]
        residuals.append(jnp.where(receiver_inside, values, 0.0))
        images.append(image)
        older, current = (current, newer)
    later, present = (adjoint_next[0], adjoint_now[0])
    for tick in reversed(range(STEPS)):
        padded = padded_2(present, (("dom", 0),), 4)
        earlier = 2.0 * present - later + model_slab * laplace(padded)
        earlier = add_at(earlier, own_row, receivers, residuals[tick])
        gradient = gradient + earlier * images[tick]
        later, present = (present, earlier)
    total = lax.psum(gradient, "shot")
    peak = lax.pmax(jnp.max(jnp.abs(total)), "dom")
    direction = total / (peak + EPSILON)
    new_model = model_slab * (1.0 - STEP_FRACTION * direction)
    return (direction, new_model)


def solution(mesh):
    placed = (
        P("dom", None, None),
        P("shot", "dom", None, None),
        P("shot", "dom", None, None),
        P("shot", "dom", None, None),
        P("shot", "dom", None, None),
        P("shot", None),
        P("shot"),
        P("shot", None),
        P("shot", None, None),
    )
    return jax.shard_map(
        on_device,
        mesh=mesh,
        in_specs=placed,
        out_specs=(P("dom", None, None), P("dom", None, None)),
        check_vma=False,
    )
```

profile of v0, /device:TPU:0, one launch (start us, length us, event | category | flops | bytes accessed | tf_op | source)
XLA Modules:
  0.0 565.6 jit_solution(65516145056497872)
XLA Ops:
  7.2 2.0 slice_bitcast_fusion.3
  10.5 6.2 %collective-permute-start.1 = (f32[4,128,128]{2,1,0:T(8,128)}, f32[4,128,128]{2,1,0:T(8,128)}, u32[]{:S(2)}, u32[]{:S(2)}) collective-permute-start(f32[4,128,128]{2,1,0:T(8,128)} %get-tuple-element.403), channel_id=1, source_target_pairs={{0,1},{1,2},{2,3},{3,4},{4,5},{5,6},{6,7},{8,9},{9,10},{10,11},{11... | collective-permute-start | bytes 786440 | tf_op jit(solution)/shard_map/ppermute | solution.py:23
  18.1 4.8 collective-permute-start.3
  55.5 9.5 %fusion.432 = (f32[16,128,128]{2,1,0:T(8,128)S(1)}, f32[16,128,128]{2,1,0:T(8,128)}) fusion(f32[1,16,128,128]{3,2,1,0:T(8,128)} %param.26, f32[16,128,128]{2,1,0:T(8,128)} %param.25, f32[1,16,128,128]{3,2,1,0:T(8,128)S(1)} %copy-done.9, f32[16,128,124]{2,1,0:T(8,128)} %get-tuple-element.385, f32[16,128,124]{2,1,0:T(8,128)} %get-tuple-element.384, ...), kind=kLoop, calls=%fused_computation.673 | loop fusion | flops 12845056 | bytes 23265280 | tf_op jit(solution)/shard_map/add | solution.py:96
  77.2 4.8 collective-permute-start.5
  84.3 7.3 %fusion.388 = f32[16,128,128]{2,1,0:T(8,128)S(1)} fusion(f32[16,128,128]{2,1,0:T(8,128)S(1)} %copy-done.13, f32[16,128,128]{2,1,0:T(8,128)S(1)} %bitcast.275, f32[4,128,128]{2,1,0:T(8,128)} %collective-permute-done.1, f32[4,128,128]{2,1,0:T(8,128)S(1)} %collective-permute-done, f32[1,16,128,128]{3,2,1,0:T(8,128)} %param.28, ...), kind=kLoop, calls=%fused_computation.596 | loop fusion | flops 12845056 | bytes 21168128 | tf_op jit(solution)/shard_map/add | solution.py:105
  94.7 5.4 multiply_add_fusion.7
  104.0 4.6 collective-permute-start.7
  111.4 6.7 %collective-permute-done.7 = f32[4,128,128]{2,1,0:T(8,128)S(1)} collective-permute-done((f32[4,128,128]{2,1,0:T(8,128)S(1)}, f32[4,128,128]{2,1,0:T(8,128)S(1)}, u32[]{:S(2)}, u32[]{:S(2)}) %collective-permute-start.7) | collective-permute-done | bytes 262176 | tf_op jit(solution)/shard_map/ppermute | solution.py:23
  118.1 7.4 %multiply_add_fusion.6 = (f32[16,128,128]{2,1,0:T(8,128)S(1)}, f32[16,128,128]{2,1,0:T(8,128)}) fusion(f32[16,128,128]{2,1,0:T(8,128)S(1)} %copy-done.14, f32[16,128,128]{2,1,0:T(8,128)S(1)} %bitcast.225, f32[16,128,128]{2,1,0:T(8,128)} %bitcast.235, f32[16,128,124]{2,1,0:T(8,128)S(1)} %get-tuple-element.349, f32[16,128,124]{2,1,0:T(8,128)S(1)} %get-tuple-element.348, ...), kind=kLoop, calls=%fused_computation.683 | loop fusion | flops 12845056 | bytes 22216704 | tf_op jit(solution)/shard_map/add | solution.py:96
  129.4 4.4 collective-permute-start.9
  137.7 6.6 %collective-permute-done.8 = f32[4,128,128]{2,1,0:T(8,128)S(1)} collective-permute-done((f32[4,128,128]{2,1,0:T(8,128)S(1)}, f32[4,128,128]{2,1,0:T(8,128)S(1)}, u32[]{:S(2)}, u32[]{:S(2)}) %collective-permute-start.8) | collective-permute-done | bytes 262176 | tf_op jit(solution)/shard_map/ppermute | solution.py:25
  144.3 5.4 multiply_add_fusion.5
  153.6 4.6 collective-permute-start.11
  162.7 7.5 %collective-permute-done.10 = f32[4,128,128]{2,1,0:T(8,128)S(1)} collective-permute-done((f32[4,128,128]{2,1,0:T(8,128)S(1)}, f32[4,128,128]{2,1,0:T(8,128)S(1)}, u32[]{:S(2)}, u32[]{:S(2)}) %collective-permute-start.10) | collective-permute-done | bytes 262176 | tf_op jit(solution)/shard_map/ppermute | solution.py:25
  170.2 5.5 multiply_add_fusion.4
  177.2 9.8 %gather_fusion.3 = f32[256]{0:T(256)S(1)} fusion(f32[262144]{0:T(1024)} %fusion.437, s32[1024]{0:T(1024)S(1)} %pad_clamp_fusion), kind=kCustom, calls=%fused_computation.3 | custom fusion | bytes 3072 | tf_op jit(solution)/shard_map/gather | solution.py:98
  201.3 3.6 collective-permute-start.13
  206.3 2.9 fusion.537
  209.2 6.1 %collective-permute-done.12 = f32[4,128,128]{2,1,0:T(8,128)S(1)} collective-permute-done((f32[4,128,128]{2,1,0:T(8,128)S(1)}, f32[4,128,128]{2,1,0:T(8,128)S(1)}, u32[]{:S(2)}, u32[]{:S(2)}) %collective-permute-start.12) | collective-permute-done | bytes 262176 | tf_op jit(solution)/shard_map/ppermute | solution.py:25
  215.3 7.6 %multiply_add_fusion.3 = (f32[16,128,128]{2,1,0:T(8,128)S(1)}, f32[16,128,128]{2,1,0:T(8,128)}) fusion(f32[16,128,128]{2,1,0:T(8,128)S(1)} %copy-done.17, f32[16,128,128]{2,1,0:T(8,128)S(1)} %bitcast.203, f32[16,128,128]{2,1,0:T(8,128)} %bitcast.40, f32[16,128,124]{2,1,0:T(8,128)S(1)} %get-tuple-element.295, f32[16,128,124]{2,1,0:T(8,128)S(1)} %get-tuple-element.294, ...), kind=kLoop, calls=%fused_computation.680 | loop fusion | flops 12845056 | bytes 22216704 | tf_op jit(solution)/shard_map/add | solution.py:96
  227.2 4.6 collective-permute-start.15
  235.6 8.2 %collective-permute-done.14 = f32[4,128,128]{2,1,0:T(8,128)S(1)} collective-permute-done((f32[4,128,128]{2,1,0:T(8,128)S(1)}, f32[4,128,128]{2,1,0:T(8,128)S(1)}, u32[]{:S(2)}, u32[]{:S(2)}) %collective-permute-start.14) | collective-permute-done | bytes 262176 | tf_op jit(solution)/shard_map/ppermute | solution.py:25
  243.8 5.5 multiply_add_fusion.2
  253.2 4.6 collective-permute-start.17
  262.3 7.5 %collective-permute-done.16 = f32[4,128,128]{2,1,0:T(8,128)S(1)} collective-permute-done((f32[4,128,128]{2,1,0:T(8,128)S(1)}, f32[4,128,128]{2,1,0:T(8,128)S(1)}, u32[]{:S(2)}, u32[]{:S(2)}) %collective-permute-start.16) | collective-permute-done | bytes 262176 | tf_op jit(solution)/shard_map/ppermute | solution.py:25
  269.8 5.6 multiply_add_fusion.1
  276.8 9.7 %gather_fusion = f32[256]{0:T(256)S(1)} fusion(f32[262144]{0:T(1024)} %fusion.440, s32[1024]{0:T(1024)S(1)} %pad_clamp_fusion), kind=kCustom, calls=%fused_computation | custom fusion | bytes 3072 | tf_op jit(solution)/shard_map/gather | solution.py:98
  286.6 2.6 scatter_fusion
  291.1 3.6 collective-permute-start.19
  296.7 2.1 collective-permute-done.19
  298.8 6.3 %collective-permute-done.18 = f32[4,128,128]{2,1,0:T(8,128)S(1)} collective-permute-done((f32[4,128,128]{2,1,0:T(8,128)S(1)}, f32[4,128,128]{2,1,0:T(8,128)S(1)}, u32[]{:S(2)}, u32[]{:S(2)}) %collective-permute-start.18) | collective-permute-done | bytes 262176 | tf_op jit(solution)/shard_map/ppermute | solution.py:25
  305.1 3.6 fusion.170
  308.7 2.6 scatter_fusion.1
  313.2 4.4 collective-permute-start.21
  319.4 2.1 collective-permute-done.21
  321.5 8.1 %collective-permute-done.20 = f32[4,128,128]{2,1,0:T(8,128)S(1)} collective-permute-done((f32[4,128,128]{2,1,0:T(8,128)S(1)}, f32[4,128,128]{2,1,0:T(8,128)S(1)}, u32[]{:S(2)}, u32[]{:S(2)}) %collective-permute-start.20) | collective-permute-done | bytes 262176 | tf_op jit(solution)/shard_map/ppermute | solution.py:25
  329.6 3.6 fusion.144
  333.2 2.6 scatter_fusion.2
  337.7 4.4 collective-permute-start.23
  344.1 2.5 collective-permute-done.23
  346.6 7.5 %collective-permute-done.22 = f32[4,128,128]{2,1,0:T(8,128)S(1)} collective-permute-done((f32[4,128,128]{2,1,0:T(8,128)S(1)}, f32[4,128,128]{2,1,0:T(8,128)S(1)}, u32[]{:S(2)}, u32[]{:S(2)}) %collective-permute-start.22) | collective-permute-done | bytes 262176 | tf_op jit(solution)/shard_map/ppermute | solution.py:25
  354.1 4.3 fusion.118
  358.4 4.3 scatter_fusion.3
  366.1 4.4 collective-permute-start.25
  372.3 2.7 collective-permute-done.25
  375.0 7.6 %collective-permute-done.24 = f32[4,128,128]{2,1,0:T(8,128)} collective-permute-done((f32[4,128,128]{2,1,0:T(8,128)S(1)}, f32[4,128,128]{2,1,0:T(8,128)}, u32[]{:S(2)}, u32[]{:S(2)}) %collective-permute-start.24) | collective-permute-done | bytes 262176 | tf_op jit(solution)/shard_map/ppermute | solution.py:25
  382.6 5.6 fusion.92
  388.2 4.3 scatter_fusion.4
  395.8 4.4 collective-permute-start.27
  404.7 7.6 %collective-permute-done.26 = f32[4,128,128]{2,1,0:T(8,128)} collective-permute-done((f32[4,128,128]{2,1,0:T(8,128)S(1)}, f32[4,128,128]{2,1,0:T(8,128)}, u32[]{:S(2)}, u32[]{:S(2)}) %collective-permute-start.26) | collective-permute-done | bytes 262176 | tf_op jit(solution)/shard_map/ppermute | solution.py:25
  412.3 5.7 %fusion.66 = f32[16,128,128]{2,1,0:T(8,128)} fusion(f32[16,128,128]{2,1,0:T(8,128)S(1)} %copy-done.24, f32[16,128,128]{2,1,0:T(8,128)S(1)} %bitcast.168, f32[4,128,128]{2,1,0:T(8,128)S(1)} %collective-permute-done.27, f32[4,128,128]{2,1,0:T(8,128)} %collective-permute-done.26, f32[16,128,124]{2,1,0:T(8,128)} %get-tuple-element.167, ...), kind=kLoop, calls=%fused_computation.274 | loop fusion | flops 12845056 | bytes 21168128 | tf_op jit(solution)/shard_map/add | solution.py:105
  418.1 4.4 scatter_fusion.5
  425.8 4.4 collective-permute-start.29
  434.7 7.6 %collective-permute-done.28 = f32[4,128,128]{2,1,0:T(8,128)} collective-permute-done((f32[4,128,128]{2,1,0:T(8,128)S(1)}, f32[4,128,128]{2,1,0:T(8,128)}, u32[]{:S(2)}, u32[]{:S(2)}) %collective-permute-start.28) | collective-permute-done | bytes 262176 | tf_op jit(solution)/shard_map/ppermute | solution.py:25
  442.3 5.7 %fusion.40 = f32[16,128,128]{2,1,0:T(8,128)} fusion(f32[16,128,128]{2,1,0:T(8,128)S(1)} %copy-done.25, f32[16,128,128]{2,1,0:T(8,128)S(1)} %bitcast.180, f32[4,128,128]{2,1,0:T(8,128)S(1)} %collective-permute-done.29, f32[4,128,128]{2,1,0:T(8,128)} %collective-permute-done.28, f32[16,128,124]{2,1,0:T(8,128)} %get-tuple-element.149, ...), kind=kLoop, calls=%fused_computation.248 | loop fusion | flops 12845056 | bytes 21168128 | tf_op jit(solution)/shard_map/add | solution.py:105
  448.0 4.4 scatter_fusion.6
  455.7 4.4 collective-permute-start.31
  464.6 7.6 %collective-permute-done.30 = f32[4,128,128]{2,1,0:T(8,128)} collective-permute-done((f32[4,128,128]{2,1,0:T(8,128)S(1)}, f32[4,128,128]{2,1,0:T(8,128)}, u32[]{:S(2)}, u32[]{:S(2)}) %collective-permute-start.30) | collective-permute-done | bytes 262176 | tf_op jit(solution)/shard_map/ppermute | solution.py:25
  472.2 5.8 %fusion.14 = f32[16,128,128]{2,1,0:T(8,128)} fusion(f32[16,128,128]{2,1,0:T(8,128)S(1)} %copy-done.26, f32[16,128,128]{2,1,0:T(8,128)S(1)} %bitcast.247, f32[4,128,128]{2,1,0:T(8,128)S(1)} %collective-permute-done.31, f32[4,128,128]{2,1,0:T(8,128)} %collective-permute-done.30, f32[16,128,124]{2,1,0:T(8,128)S(1)} %get-tuple-element.131, ...), kind=kLoop, calls=%fused_computation.222 | loop fusion | flops 12845056 | bytes 21168128 | tf_op jit(solution)/shard_map/add | solution.py:105
  477.9 4.4 scatter_fusion.7
  482.4 7.7 %multiply_add_fusion = f32[16,128,128]{2,1,0:T(8,128)} fusion(f32[16,128,128]{2,1,0:T(8,128)} %bitcast.277, f32[16,128,128]{2,1,0:T(8,128)} %get-tuple-element.115, f32[16,128,128]{2,1,0:T(8,128)} %bitcast.238, f32[16,128,128]{2,1,0:T(8,128)} %get-tuple-element.113, f32[16,128,128]{2,1,0:T(8,128)} %bitcast.171, f32[16,128,128]{2,1,0:T(8,128)} %get-tuple-element.111, ...), kind=kLoop, calls=%fused_computation.677 | loop fusion | flops 3932160 | bytes 17825792 | tf_op jit(solution)/shard_map/add | solution.py:107
  490.1 42.0 %all-reduce.258.cloned.1.call-done = f32[16,128,128]{2,1,0:T(8,128)} async-done(((f32[16,128,128]{2,1,0:T(8,128)}), f32[16,128,128]{2,1,0:T(8,128)}) %all-reduce.258.cloned.1.call-update) | async-done | bytes 1048592 | tf_op jit(solution)/shard_map/psum | solution.py:109
  534.1 22.0 %pmax.7 = f32[]{:T(128)} all-reduce(f32[]{:T(128)} %abs_reduce_fusion), channel_id=1, replica_groups=mesh['shot'=4,'dom'=8] {'dom'}, use_global_device_ids=true, to_apply=%region_10.11 | all-reduce | flops 1 | bytes 8 | tf_op jit(solution)/shard_map/pmax | solution.py:110
  (295 shorter events, 147.8 us)
Async XLA Ops:
  7.2 9.6 %copy-start.9 = (f32[1,16,128,128]{3,2,1,0:T(8,128)S(1)}, f32[1,16,128,128]{3,2,1,0:T(8,128)}, u32[]{:S(2)}) copy-start(f32[1,16,128,128]{3,2,1,0:T(8,128)} %param.27) | copy-start | bytes 3145732
  7.2 15.7 %copy-start.11 = (f32[1,16,128,128]{3,2,1,0:T(8,128)S(1)}, f32[1,16,128,128]{3,2,1,0:T(8,128)}, u32[]{:S(2)}) copy-start(f32[1,16,128,128]{3,2,1,0:T(8,128)} %param.29) | copy-start | bytes 3145732
  7.2 15.7 %copy-start.48 = (s32[1,256]{1,0:T(1,128)S(1)}, s32[1,256]{1,0:T(1,128)}, u32[]{:S(2)}) copy-start(s32[1,256]{1,0:T(1,128)} %param.32) | copy-start | bytes 3076
  7.2 524.9 %all-reduce.258.cloned.1.call-start = ((), (), s32[]{:S(2)}) async-start(), calls=%async_computation | async-start | bytes 2097152 | tf_op jit(solution)/shard_map/psum | solution.py:109
  9.2 74.9 %collective-permute-start = (f32[4,128,128]{2,1,0:T(8,128)}, f32[4,128,128]{2,1,0:T(8,128)S(1)}, u32[]{:S(2)}, u32[]{:S(2)}) collective-permute-start(f32[4,128,128]{2,1,0:T(8,128)} %get-tuple-element.402), channel_id=1, source_target_pairs={{1,0},{2,1},{3,2},{4,3},{5,4},{6,5},{7,6},{9,8},{10,9},{11,10},{12... | collective-permute-start | bytes 786440 | tf_op jit(solution)/shard_map/ppermute | solution.py:25
  10.5 73.7 %collective-permute-start.1 = (f32[4,128,128]{2,1,0:T(8,128)}, f32[4,128,128]{2,1,0:T(8,128)}, u32[]{:S(2)}, u32[]{:S(2)}) collective-permute-start(f32[4,128,128]{2,1,0:T(8,128)} %get-tuple-element.403), channel_id=1, source_target_pairs={{0,1},{1,2},{2,3},{3,4},{4,5},{5,6},{6,7},{8,9},{9,10},{10,11},{11... | collective-permute-start | bytes 786440 | tf_op jit(solution)/shard_map/ppermute | solution.py:23
  16.8 38.0 %collective-permute-start.2 = (f32[4,128,128]{2,1,0:T(8,128)S(1)}, f32[4,128,128]{2,1,0:T(8,128)S(1)}, u32[]{:S(2)}, u32[]{:S(2)}) collective-permute-start(f32[4,128,128]{2,1,0:T(8,128)S(1)} %get-tuple-element.368), channel_id=1, source_target_pairs={{1,0},{2,1},{3,2},{4,3},{5,4},{6,5},{7,6},{9,8},{10,9},{11,10},{12... | collective-permute-start | bytes 786440 | tf_op jit(solution)/shard_map/ppermute | solution.py:25
  18.1 36.7 %collective-permute-start.3 = (f32[4,128,128]{2,1,0:T(8,128)S(1)}, f32[4,128,128]{2,1,0:T(8,128)S(1)}, u32[]{:S(2)}, u32[]{:S(2)}) collective-permute-start(f32[4,128,128]{2,1,0:T(8,128)S(1)} %get-tuple-element.369), channel_id=1, source_target_pairs={{0,1},{1,2},{2,3},{3,4},{4,5},{5,6},{6,7},{8,9},{9,10},{10,11},{11... | collective-permute-start | bytes 786440 | tf_op jit(solution)/shard_map/ppermute | solution.py:23
  77.2 16.1 %collective-permute-start.5 = (f32[4,128,128]{2,1,0:T(8,128)}, f32[4,128,128]{2,1,0:T(8,128)S(1)}, u32[]{:S(2)}, u32[]{:S(2)}) collective-permute-start(f32[4,128,128]{2,1,0:T(8,128)} %bitcast.18), channel_id=1, source_target_pairs={{0,1},{1,2},{2,3},{3,4},{4,5},{5,6},{6,7},{8,9},{9,10},{10,11},{11... | collective-permute-start | bytes 786440 | tf_op jit(solution)/shard_map/ppermute | solution.py:23
  82.1 11.2 %collective-permute-start.4 = (f32[4,128,128]{2,1,0:T(8,128)}, f32[4,128,128]{2,1,0:T(8,128)S(1)}, u32[]{:S(2)}, u32[]{:S(2)}) collective-permute-start(f32[4,128,128]{2,1,0:T(8,128)} %bitcast.17), channel_id=1, source_target_pairs={{1,0},{2,1},{3,2},{4,3},{5,4},{6,5},{7,6},{9,8},{10,9},{11,10},{12... | collective-permute-start | bytes 786440 | tf_op jit(solution)/shard_map/ppermute | solution.py:25
  84.2 9.1 %copy-start.32 = (f32[16,125,128]{2,1,0:T(8,128)S(1)}, f32[16,125,128]{2,1,0:T(8,128)}, u32[]{:S(2)}) copy-start(f32[16,125,128]{2,1,0:T(8,128)} %get-tuple-element.357) | copy-start | bytes 3072004
  84.3 9.1 %copy-start.33 = (f32[16,128,126]{2,1,0:T(8,128)S(1)}, f32[16,128,126]{2,1,0:T(8,128)}, u32[]{:S(2)}) copy-start(f32[16,128,126]{2,1,0:T(8,128)} %get-tuple-element.362) | copy-start | bytes 3096580
  84.3 9.1 %copy-start.34 = (f32[16,128,126]{2,1,0:T(8,128)S(1)}, f32[16,128,126]{2,1,0:T(8,128)}, u32[]{:S(2)}) copy-start(f32[16,128,126]{2,1,0:T(8,128)} %get-tuple-element.363) | copy-start | bytes 3096580
  84.3 9.1 %copy-start.35 = (f32[16,126,128]{2,1,0:T(8,128)S(1)}, f32[16,126,128]{2,1,0:T(8,128)}, u32[]{:S(2)}) copy-start(f32[16,126,128]{2,1,0:T(8,128)} %get-tuple-element.354) | copy-start | bytes 3096580
  84.3 9.1 %copy-start.36 = (f32[16,126,128]{2,1,0:T(8,128)S(1)}, f32[16,126,128]{2,1,0:T(8,128)}, u32[]{:S(2)}) copy-start(f32[16,126,128]{2,1,0:T(8,128)} %get-tuple-element.355) | copy-start | bytes 3096580
  84.3 9.1 %copy-start.37 = (f32[16,124,128]{2,1,0:T(8,128)S(1)}, f32[16,124,128]{2,1,0:T(8,128)}, u32[]{:S(2)}) copy-start(f32[16,124,128]{2,1,0:T(8,128)} %get-tuple-element.358) | copy-start | bytes 3047428
  84.3 9.1 %copy-start.38 = (f32[16,124,128]{2,1,0:T(8,128)S(1)}, f32[16,124,128]{2,1,0:T(8,128)}, u32[]{:S(2)}) copy-start(f32[16,124,128]{2,1,0:T(8,128)} %get-tuple-element.359) | copy-start | bytes 3047428
  100.3 9.7 %copy-start.6 = (f32[262144]{0:T(1024)}, f32[262144]{0:T(1024)S(1)}, u32[]{:S(2)}) copy-start(f32[262144]{0:T(1024)S(1)} %fusion.434) | copy-start | bytes 3145732
  104.0 14.0 %collective-permute-start.7 = (f32[4,128,128]{2,1,0:T(8,128)S(1)}, f32[4,128,128]{2,1,0:T(8,128)S(1)}, u32[]{:S(2)}, u32[]{:S(2)}) collective-permute-start(f32[4,128,128]{2,1,0:T(8,128)S(1)} %bitcast.291), channel_id=1, source_target_pairs={{0,1},{1,2},{2,3},{3,4},{4,5},{5,6},{6,7},{8,9},{9,10},{10,11},{11... | collective-permute-start | bytes 786440 | tf_op jit(solution)/shard_map/ppermute | solution.py:23
  108.6 9.5 %copy-start.14 = (f32[16,128,128]{2,1,0:T(8,128)S(1)}, f32[16,128,128]{2,1,0:T(8,128)}, u32[]{:S(2)}) copy-start(f32[16,128,128]{2,1,0:T(8,128)} %param.25) | copy-start | bytes 3145732
  108.6 9.5 %collective-permute-start.6 = (f32[4,128,128]{2,1,0:T(8,128)S(1)}, f32[4,128,128]{2,1,0:T(8,128)S(1)}, u32[]{:S(2)}, u32[]{:S(2)}) collective-permute-start(f32[4,128,128]{2,1,0:T(8,128)S(1)} %bitcast.278), channel_id=1, source_target_pairs={{1,0},{2,1},{3,2},{4,3},{5,4},{6,5},{7,6},{9,8},{10,9},{11,10},{12... | collective-permute-start | bytes 786440 | tf_op jit(solution)/shard_map/ppermute | solution.py:25
  129.4 8.3 %collective-permute-start.9 = (f32[4,128,128]{2,1,0:T(8,128)S(1)}, f32[4,128,128]{2,1,0:T(8,128)S(1)}, u32[]{:S(2)}, u32[]{:S(2)}) collective-permute-start(f32[4,128,128]{2,1,0:T(8,128)S(1)} %bitcast.292), channel_id=1, source_target_pairs={{0,1},{1,2},{2,3},{3,4},{4,5},{5,6},{6,7},{8,9},{9,10},{10,11},{11... | collective-permute-start | bytes 786440 | tf_op jit(solution)/shard_map/ppermute | solution.py:23
  133.8 10.4 %copy-start.7 = (f32[262144]{0:T(1024)S(1)}, f32[262144]{0:T(1024)}, u32[]{:S(2)}) copy-start(f32[262144]{0:T(1024)} %copy-done.6) | copy-start | bytes 3145732
  133.8 10.4 %copy-start.15 = (f32[16,128,128]{2,1,0:T(8,128)S(1)}, f32[16,128,128]{2,1,0:T(8,128)}, u32[]{:S(2)}) copy-start(f32[16,128,128]{2,1,0:T(8,128)} %param.25) | copy-start | bytes 3145732
  133.8 10.4 %collective-permute-start.8 = (f32[4,128,128]{2,1,0:T(8,128)S(1)}, f32[4,128,128]{2,1,0:T(8,128)S(1)}, u32[]{:S(2)}, u32[]{:S(2)}) collective-permute-start(f32[4,128,128]{2,1,0:T(8,128)S(1)} %bitcast.279), channel_id=1, source_target_pairs={{1,0},{2,1},{3,2},{4,3},{5,4},{6,5},{7,6},{9,8},{10,9},{11,10},{12... | collective-permute-start | bytes 786440 | tf_op jit(solution)/shard_map/ppermute | solution.py:25
  153.6 9.1 %collective-permute-start.11 = (f32[4,128,128]{2,1,0:T(8,128)S(1)}, f32[4,128,128]{2,1,0:T(8,128)S(1)}, u32[]{:S(2)}, u32[]{:S(2)}) collective-permute-start(f32[4,128,128]{2,1,0:T(8,128)S(1)} %bitcast.293), channel_id=1, source_target_pairs={{0,1},{1,2},{2,3},{3,4},{4,5},{5,6},{6,7},{8,9},{9,10},{10,11},{11... | collective-permute-start | bytes 786440 | tf_op jit(solution)/shard_map/ppermute | solution.py:23
  158.1 12.1 %copy-start.16 = (f32[16,128,128]{2,1,0:T(8,128)S(1)}, f32[16,128,128]{2,1,0:T(8,128)}, u32[]{:S(2)}) copy-start(f32[16,128,128]{2,1,0:T(8,128)} %param.25) | copy-start | bytes 3145732
  158.1 12.1 %collective-permute-start.10 = (f32[4,128,128]{2,1,0:T(8,128)S(1)}, f32[4,128,128]{2,1,0:T(8,128)S(1)}, u32[]{:S(2)}, u32[]{:S(2)}) collective-permute-start(f32[4,128,128]{2,1,0:T(8,128)S(1)} %bitcast.280), channel_id=1, source_target_pairs={{1,0},{2,1},{3,2},{4,3},{5,4},{6,5},{7,6},{9,8},{10,9},{11,10},{12... | collective-permute-start | bytes 786440 | tf_op jit(solution)/shard_map/ppermute | solution.py:25
  201.3 7.9 %collective-permute-start.13 = (f32[4,128,128]{2,1,0:T(8,128)S(1)}, f32[4,128,128]{2,1,0:T(8,128)S(1)}, u32[]{:S(2)}, u32[]{:S(2)}) collective-permute-start(f32[4,128,128]{2,1,0:T(8,128)S(1)} %bitcast.294), channel_id=1, source_target_pairs={{0,1},{1,2},{2,3},{3,4},{4,5},{5,6},{6,7},{8,9},{9,10},{10,11},{11... | collective-permute-start | bytes 786440 | tf_op jit(solution)/shard_map/ppermute | solution.py:23
  204.9 10.5 %copy-start.17 = (f32[16,128,128]{2,1,0:T(8,128)S(1)}, f32[16,128,128]{2,1,0:T(8,128)}, u32[]{:S(2)}) copy-start(f32[16,128,128]{2,1,0:T(8,128)} %param.25) | copy-start | bytes 3145732
  204.9 10.4 %collective-permute-start.12 = (f32[4,128,128]{2,1,0:T(8,128)S(1)}, f32[4,128,128]{2,1,0:T(8,128)S(1)}, u32[]{:S(2)}, u32[]{:S(2)}) collective-permute-start(f32[4,128,128]{2,1,0:T(8,128)S(1)} %bitcast.281), channel_id=1, source_target_pairs={{1,0},{2,1},{3,2},{4,3},{5,4},{6,5},{7,6},{9,8},{10,9},{11,10},{12... | collective-permute-start | bytes 786440 | tf_op jit(solution)/shard_map/ppermute | solution.py:25
  227.2 8.4 %collective-permute-start.15 = (f32[4,128,128]{2,1,0:T(8,128)S(1)}, f32[4,128,128]{2,1,0:T(8,128)S(1)}, u32[]{:S(2)}, u32[]{:S(2)}) collective-permute-start(f32[4,128,128]{2,1,0:T(8,128)S(1)} %bitcast.295), channel_id=1, source_target_pairs={{0,1},{1,2},{2,3},{3,4},{4,5},{5,6},{6,7},{8,9},{9,10},{10,11},{11... | collective-permute-start | bytes 786440 | tf_op jit(solution)/shard_map/ppermute | solution.py:23
  231.8 12.1 %copy-start.18 = (f32[16,128,128]{2,1,0:T(8,128)S(1)}, f32[16,128,128]{2,1,0:T(8,128)}, u32[]{:S(2)}) copy-start(f32[16,128,128]{2,1,0:T(8,128)} %param.25) | copy-start | bytes 3145732
  231.8 12.1 %collective-permute-start.14 = (f32[4,128,128]{2,1,0:T(8,128)S(1)}, f32[4,128,128]{2,1,0:T(8,128)S(1)}, u32[]{:S(2)}, u32[]{:S(2)}) collective-permute-start(f32[4,128,128]{2,1,0:T(8,128)S(1)} %bitcast.282), channel_id=1, source_target_pairs={{1,0},{2,1},{3,2},{4,3},{5,4},{6,5},{7,6},{9,8},{10,9},{11,10},{12... | collective-permute-start | bytes 786440 | tf_op jit(solution)/shard_map/ppermute | solution.py:25
  253.2 9.1 %collective-permute-start.17 = (f32[4,128,128]{2,1,0:T(8,128)S(1)}, f32[4,128,128]{2,1,0:T(8,128)S(1)}, u32[]{:S(2)}, u32[]{:S(2)}) collective-permute-start(f32[4,128,128]{2,1,0:T(8,128)S(1)} %bitcast.296), channel_id=1, source_target_pairs={{0,1},{1,2},{2,3},{3,4},{4,5},{5,6},{6,7},{8,9},{9,10},{10,11},{11... | collective-permute-start | bytes 786440 | tf_op jit(solution)/shard_map/ppermute | solution.py:23
  257.7 12.1 %copy-start.19 = (f32[16,128,128]{2,1,0:T(8,128)S(1)}, f32[16,128,128]{2,1,0:T(8,128)}, u32[]{:S(2)}) copy-start(f32[16,128,128]{2,1,0:T(8,128)} %param.25) | copy-start | bytes 3145732
  257.7 12.1 %collective-permute-start.16 = (f32[4,128,128]{2,1,0:T(8,128)S(1)}, f32[4,128,128]{2,1,0:T(8,128)S(1)}, u32[]{:S(2)}, u32[]{:S(2)}) collective-permute-start(f32[4,128,128]{2,1,0:T(8,128)S(1)} %bitcast.283), channel_id=1, source_target_pairs={{1,0},{2,1},{3,2},{4,3},{5,4},{6,5},{7,6},{9,8},{10,9},{11,10},{12... | collective-permute-start | bytes 786440 | tf_op jit(solution)/shard_map/ppermute | solution.py:25
  291.1 7.6 %collective-permute-start.19 = (f32[4,128,128]{2,1,0:T(8,128)S(1)}, f32[4,128,128]{2,1,0:T(8,128)S(1)}, u32[]{:S(2)}, u32[]{:S(2)}) collective-permute-start(f32[4,128,128]{2,1,0:T(8,128)S(1)} %bitcast.297), channel_id=1, source_target_pairs={{0,1},{1,2},{2,3},{3,4},{4,5},{5,6},{6,7},{8,9},{9,10},{10,11},{11... | collective-permute-start | bytes 786440 | tf_op jit(solution)/shard_map/ppermute | solution.py:23
  294.7 10.4 %copy-start.12 = (f32[1,16,128,128]{3,2,1,0:T(8,128)S(1)}, f32[1,16,128,128]{3,2,1,0:T(8,128)}, u32[]{:S(2)}) copy-start(f32[1,16,128,128]{3,2,1,0:T(8,128)} %param.29) | copy-start | bytes 3145732
  294.7 10.4 %copy-start.20 = (f32[16,128,128]{2,1,0:T(8,128)S(1)}, f32[16,128,128]{2,1,0:T(8,128)}, u32[]{:S(2)}) copy-start(f32[16,128,128]{2,1,0:T(8,128)} %param.25) | copy-start | bytes 3145732
  294.7 10.3 %collective-permute-start.18 = (f32[4,128,128]{2,1,0:T(8,128)S(1)}, f32[4,128,128]{2,1,0:T(8,128)S(1)}, u32[]{:S(2)}, u32[]{:S(2)}) collective-permute-start(f32[4,128,128]{2,1,0:T(8,128)S(1)} %bitcast.284), channel_id=1, source_target_pairs={{1,0},{2,1},{3,2},{4,3},{5,4},{6,5},{7,6},{9,8},{10,9},{11,10},{12... | collective-permute-start | bytes 786440 | tf_op jit(solution)/shard_map/ppermute | solution.py:25
  313.2 8.3 %collective-permute-start.21 = (f32[4,128,128]{2,1,0:T(8,128)S(1)}, f32[4,128,128]{2,1,0:T(8,128)S(1)}, u32[]{:S(2)}, u32[]{:S(2)}) collective-permute-start(f32[4,128,128]{2,1,0:T(8,128)S(1)} %bitcast.298), channel_id=1, source_target_pairs={{0,1},{1,2},{2,3},{3,4},{4,5},{5,6},{6,7},{8,9},{9,10},{10,11},{11... | collective-permute-start | bytes 786440 | tf_op jit(solution)/shard_map/ppermute | solution.py:23
  317.6 12.0 %copy-start.21 = (f32[16,128,128]{2,1,0:T(8,128)S(1)}, f32[16,128,128]{2,1,0:T(8,128)}, u32[]{:S(2)}) copy-start(f32[16,128,128]{2,1,0:T(8,128)} %param.25) | copy-start | bytes 3145732
  317.6 12.0 %collective-permute-start.20 = (f32[4,128,128]{2,1,0:T(8,128)S(1)}, f32[4,128,128]{2,1,0:T(8,128)S(1)}, u32[]{:S(2)}, u32[]{:S(2)}) collective-permute-start(f32[4,128,128]{2,1,0:T(8,128)S(1)} %bitcast.285), channel_id=1, source_target_pairs={{1,0},{2,1},{3,2},{4,3},{5,4},{6,5},{7,6},{9,8},{10,9},{11,10},{12... | collective-permute-start | bytes 786440 | tf_op jit(solution)/shard_map/ppermute | solution.py:25
  337.7 8.9 %collective-permute-start.23 = (f32[4,128,128]{2,1,0:T(8,128)S(1)}, f32[4,128,128]{2,1,0:T(8,128)S(1)}, u32[]{:S(2)}, u32[]{:S(2)}) collective-permute-start(f32[4,128,128]{2,1,0:T(8,128)S(1)} %bitcast.299), channel_id=1, source_target_pairs={{0,1},{1,2},{2,3},{3,4},{4,5},{5,6},{6,7},{8,9},{9,10},{10,11},{11... | collective-permute-start | bytes 786440 | tf_op jit(solution)/shard_map/ppermute | solution.py:23
  342.1 12.0 %copy-start.22 = (f32[16,128,128]{2,1,0:T(8,128)S(1)}, f32[16,128,128]{2,1,0:T(8,128)}, u32[]{:S(2)}) copy-start(f32[16,128,128]{2,1,0:T(8,128)} %param.25) | copy-start | bytes 3145732
  342.1 12.0 %collective-permute-start.22 = (f32[4,128,128]{2,1,0:T(8,128)S(1)}, f32[4,128,128]{2,1,0:T(8,128)S(1)}, u32[]{:S(2)}, u32[]{:S(2)}) collective-permute-start(f32[4,128,128]{2,1,0:T(8,128)S(1)} %bitcast.286), channel_id=1, source_target_pairs={{1,0},{2,1},{3,2},{4,3},{5,4},{6,5},{7,6},{9,8},{10,9},{11,10},{12... | collective-permute-start | bytes 786440 | tf_op jit(solution)/shard_map/ppermute | solution.py:25
  366.1 8.9 %collective-permute-start.25 = (f32[4,128,128]{2,1,0:T(8,128)S(1)}, f32[4,128,128]{2,1,0:T(8,128)S(1)}, u32[]{:S(2)}, u32[]{:S(2)}) collective-permute-start(f32[4,128,128]{2,1,0:T(8,128)S(1)} %bitcast.300), channel_id=1, source_target_pairs={{0,1},{1,2},{2,3},{3,4},{4,5},{5,6},{6,7},{8,9},{9,10},{10,11},{11... | collective-permute-start | bytes 786440 | tf_op jit(solution)/shard_map/ppermute | solution.py:23
  370.5 12.1 %copy-start.23 = (f32[16,128,128]{2,1,0:T(8,128)S(1)}, f32[16,128,128]{2,1,0:T(8,128)}, u32[]{:S(2)}) copy-start(f32[16,128,128]{2,1,0:T(8,128)} %param.25) | copy-start | bytes 3145732
  370.5 12.1 %collective-permute-start.24 = (f32[4,128,128]{2,1,0:T(8,128)S(1)}, f32[4,128,128]{2,1,0:T(8,128)}, u32[]{:S(2)}, u32[]{:S(2)}) collective-permute-start(f32[4,128,128]{2,1,0:T(8,128)S(1)} %bitcast.287), channel_id=1, source_target_pairs={{1,0},{2,1},{3,2},{4,3},{5,4},{6,5},{7,6},{9,8},{10,9},{11,10},{12... | collective-permute-start | bytes 786440 | tf_op jit(solution)/shard_map/ppermute | solution.py:25
  395.8 8.9 %collective-permute-start.27 = (f32[4,128,128]{2,1,0:T(8,128)S(1)}, f32[4,128,128]{2,1,0:T(8,128)S(1)}, u32[]{:S(2)}, u32[]{:S(2)}) collective-permute-start(f32[4,128,128]{2,1,0:T(8,128)S(1)} %bitcast.301), channel_id=1, source_target_pairs={{0,1},{1,2},{2,3},{3,4},{4,5},{5,6},{6,7},{8,9},{9,10},{10,11},{11... | collective-permute-start | bytes 786440 | tf_op jit(solution)/shard_map/ppermute | solution.py:23
  400.2 12.1 %copy-start.1 = (f32[262144]{0:T(1024)S(1)}, f32[262144]{0:T(1024)}, u32[]{:S(2)}) copy-start(f32[262144]{0:T(1024)} %scatter_fusion.3) | copy-start | bytes 3145732
  400.2 12.1 %copy-start.24 = (f32[16,128,128]{2,1,0:T(8,128)S(1)}, f32[16,128,128]{2,1,0:T(8,128)}, u32[]{:S(2)}) copy-start(f32[16,128,128]{2,1,0:T(8,128)} %param.25) | copy-start | bytes 3145732
  400.2 12.1 %collective-permute-start.26 = (f32[4,128,128]{2,1,0:T(8,128)S(1)}, f32[4,128,128]{2,1,0:T(8,128)}, u32[]{:S(2)}, u32[]{:S(2)}) collective-permute-start(f32[4,128,128]{2,1,0:T(8,128)S(1)} %bitcast.288), channel_id=1, source_target_pairs={{1,0},{2,1},{3,2},{4,3},{5,4},{6,5},{7,6},{9,8},{10,9},{11,10},{12... | collective-permute-start | bytes 786440 | tf_op jit(solution)/shard_map/ppermute | solution.py:25
  425.8 8.9 %collective-permute-start.29 = (f32[4,128,128]{2,1,0:T(8,128)S(1)}, f32[4,128,128]{2,1,0:T(8,128)S(1)}, u32[]{:S(2)}, u32[]{:S(2)}) collective-permute-start(f32[4,128,128]{2,1,0:T(8,128)S(1)} %bitcast.302), channel_id=1, source_target_pairs={{0,1},{1,2},{2,3},{3,4},{4,5},{5,6},{6,7},{8,9},{9,10},{10,11},{11... | collective-permute-start | bytes 786440 | tf_op jit(solution)/shard_map/ppermute | solution.py:23
  430.2 12.1 %copy-start.3 = (f32[262144]{0:T(1024)S(1)}, f32[262144]{0:T(1024)}, u32[]{:S(2)}) copy-start(f32[262144]{0:T(1024)} %scatter_fusion.4) | copy-start | bytes 3145732
  430.2 12.1 %copy-start.25 = (f32[16,128,128]{2,1,0:T(8,128)S(1)}, f32[16,128,128]{2,1,0:T(8,128)}, u32[]{:S(2)}) copy-start(f32[16,128,128]{2,1,0:T(8,128)} %param.25) | copy-start | bytes 3145732
  430.2 12.1 %collective-permute-start.28 = (f32[4,128,128]{2,1,0:T(8,128)S(1)}, f32[4,128,128]{2,1,0:T(8,128)}, u32[]{:S(2)}, u32[]{:S(2)}) collective-permute-start(f32[4,128,128]{2,1,0:T(8,128)S(1)} %bitcast.289), channel_id=1, source_target_pairs={{1,0},{2,1},{3,2},{4,3},{5,4},{6,5},{7,6},{9,8},{10,9},{11,10},{12... | collective-permute-start | bytes 786440 | tf_op jit(solution)/shard_map/ppermute | solution.py:25
  455.7 8.9 %collective-permute-start.31 = (f32[4,128,128]{2,1,0:T(8,128)S(1)}, f32[4,128,128]{2,1,0:T(8,128)S(1)}, u32[]{:S(2)}, u32[]{:S(2)}) collective-permute-start(f32[4,128,128]{2,1,0:T(8,128)S(1)} %bitcast.303), channel_id=1, source_target_pairs={{0,1},{1,2},{2,3},{3,4},{4,5},{5,6},{6,7},{8,9},{9,10},{10,11},{11... | collective-permute-start | bytes 786440 | tf_op jit(solution)/shard_map/ppermute | solution.py:23
  460.1 12.1 %copy-start.5 = (f32[262144]{0:T(1024)S(1)}, f32[262144]{0:T(1024)}, u32[]{:S(2)}) copy-start(f32[262144]{0:T(1024)} %scatter_fusion.5) | copy-start | bytes 3145732
  460.1 12.1 %copy-start.26 = (f32[16,128,128]{2,1,0:T(8,128)S(1)}, f32[16,128,128]{2,1,0:T(8,128)}, u32[]{:S(2)}) copy-start(f32[16,128,128]{2,1,0:T(8,128)} %param.25) | copy-start | bytes 3145732
  460.1 12.1 %collective-permute-start.30 = (f32[4,128,128]{2,1,0:T(8,128)S(1)}, f32[4,128,128]{2,1,0:T(8,128)}, u32[]{:S(2)}, u32[]{:S(2)}) collective-permute-start(f32[4,128,128]{2,1,0:T(8,128)S(1)} %bitcast.290), channel_id=1, source_target_pairs={{1,0},{2,1},{3,2},{4,3},{5,4},{6,5},{7,6},{9,8},{10,9},{11,10},{12... | collective-permute-start | bytes 786440 | tf_op jit(solution)/shard_map/ppermute | solution.py:25
  490.1 66.6 %copy-start.27 = (f32[16,128,128]{2,1,0:T(8,128)S(1)}, f32[16,128,128]{2,1,0:T(8,128)}, u32[]{:S(2)}) copy-start(f32[16,128,128]{2,1,0:T(8,128)} %param.25) | copy-start | bytes 3145732
  532.1 24.6 %copy-start.28 = (f32[16,128,128]{2,1,0:T(8,128)S(1)}, f32[16,128,128]{2,1,0:T(8,128)}, u32[]{:S(2)}) copy-start(f32[16,128,128]{2,1,0:T(8,128)} %all-reduce.258.cloned.1.call-done) | copy-start | bytes 3145732
  (18 other events, 53.4 us)
Sparse Core Ops, SparseCore 0:
  490.3 41.8 all-reduce.257
where the time goes:
time: 575 us; the launch traced here: 566 us
  waiting for transfers between devices  156 us (27%)
  other arithmetic  139 us (24%)
  local copies, waits for them, and re-layouts  131 us (23%)
  starting transfers between devices  96 us (17%)
  between operations  22.4 us (4%)
  blocking collectives  22 us (4%)
    ppermute x16, waiting for transfers between devices, padded_2(): lax.ppermute(head, axis, [((i + 1) % count, i) for i in range(ends)])  88.4 us
    slice x128, local copies, waits for them, and re-layouts, shifted(): lax.slice_in_dim(field, offset, length, axis=axis)  88.1 us
    ppermute x16, starting transfers between devices, padded_2(): lax.ppermute(tail, axis, [(i, (i + 1) % count) for i in range(ends)])  72 us
    add x8, other arithmetic, on_device(): newer = 2.0 * current - older + model_slab * image  51.9 us
    psum x1, waiting for transfers between devices, on_device(): total = lax.psum(gradient, 'shot')  42 us
    add x8, other arithmetic, on_device(): earlier = 2.0 * present - later + model_slab * laplace(padded)  41.5 us
    scatter-add x16, other arithmetic, add_at(): return field.reshape(-1).at[slots].add(values).reshape(field.shape)  33.9 us
    gather x8, local copies, waits for them, and re-layouts, on_device(): values = newer.reshape(-1)[receiver_slots] - observed[0, tick]  29.9 us
  transfers between devices with their start and end apart: 33, of which 25 were waited for; matrix products, arithmetic and copies ran while one was open for 13% of the time, Pallas kernels for 0%

commit v1 on v0

v1 whole, which is shorter than its diff:
```python
import functools
import math

import jax
import jax.numpy as jnp
from jax import lax
from jax.experimental import pallas as pl
from jax.experimental.pallas import tpu as pltpu
from jax.sharding import PartitionSpec as P

STEPS = 8
COEFFS = (8.0 / 5.0, -1.0 / 5.0, 8.0 / 315.0, -1.0 / 560.0)
CENTRE = -205.0 / 72.0
BAND = (8064.0, -1008.0, 128.0, -9.0)
BAND_SCALE = 1.0 / 5040.0
STEP_FRACTION = 0.1
EPSILON = 1e-06
MESH = pl.DeviceIdType.MESH
F32, BF16 = jnp.float32, jnp.bfloat16


def pieces(value):
    high = value.astype(BF16)
    rest = value - high.astype(F32)
    middle = rest.astype(BF16)
    low = (rest - middle.astype(F32)).astype(BF16)
    return high, middle, low


def kernel(
    shots, doms,
    pack_in, model_in, wprev_in, wnow_in, anext_in, anow_in,
    direction_ref, new_model_ref,
    wave, adj, images, sources, counts, model, grad, pack, targets, band, spot, other, parts, total,
    own_model, tops,
    swap_send, swap_recv, halo_send, halo_recv, far_send, far_recv, model_send, model_recv,
    sum_send, sum_recv, part_send, part_recv, all_send, all_recv, core_send, core_recv,
    top_send, top_recv, own_sem,
):
    rows, ny, nz = model.shape
    rec = pack.shape[2]
    shot, dom = lax.axis_index("shot"), lax.axis_index("dom")
    group, core = shot // 2, shot % 2
    pair, half = dom // 2, dom % 2
    groups = shots // 2
    chunk = rows // groups
    pieces_of = math.gcd(4, chunk)
    depth = chunk // pieces_of
    slab = 2 * pair + core
    moves = core != half
    stays = core == half
    partner = {"shot": 2 * group + (1 - core), "dom": 2 * pair + (1 - half)}
    across = {"shot": shot, "dom": 2 * pair + (1 - half)}
    beside = {"shot": 2 * group + (1 - core), "dom": dom}
    far_side, near_side = core, 1 - core

    def has(side):
        return jnp.where(side == 0, slab > 0, slab < doms - 1)

    def toward(side):
        step = jnp.where(side == core, jnp.where(side == 0, -2, 2), 0)
        return {"shot": 2 * group + (1 - core), "dom": dom + step}

    for buf in (wave, adj):
        def clear(i, carry, buf=buf):
            for slot in range(2):
                buf[slot, i, 0:8, :] = jnp.zeros((8, nz), F32)
                buf[slot, i, ny + 8 : ny + 16, :] = jnp.zeros((8, nz), F32)
            return carry

        lax.fori_loop(0, rows + 8, clear, 0)

        def clear_halo(i, carry, buf=buf):
            for slot in range(2):
                buf[slot, i, 8 : ny + 8, :] = jnp.zeros((ny, nz), F32)
                buf[slot, rows + 4 + i, 8 : ny + 8, :] = jnp.zeros((ny, nz), F32)
            return carry

        lax.fori_loop(0, 4, clear_halo, 0)

    barrier = pltpu.get_barrier_semaphore()

    def greet(device):
        pl.semaphore_signal(barrier, inc=1, device_id=device, device_id_type=MESH)

    def member(n):
        return {"shot": 2 * group + n % 2, "dom": n // 2}

    me = 2 * dom + core

    def meet(n, carry):
        @pl.when(n != me)
        def _():
            greet(member(n))

        return carry

    lax.fori_loop(0, 2 * doms, meet, 0)
    for o in range(1, groups):
        greet({"shot": 2 * lax.rem(group + o, groups) + core, "dom": dom})
    pl.semaphore_wait(barrier, 2 * doms - 1 + groups - 1)

    def block(ref, index):
        return ref.at[pl.ds(index * chunk, chunk)]

    def own(buf, slot):
        return buf.at[slot, pl.ds(4, rows), pl.ds(8, ny), :]

    swaps = (
        (pack_in, pack),
        (wnow_in, own(wave, 0)),
        (wprev_in, own(wave, 1)),
        (model_in, model),
        (anow_in, own(adj, 0)),
        (anext_in, own(adj, 1)),
    )

    def remote(i):
        src, dst = swaps[i]
        if i == 3:
            src, dst = block(src, group), block(dst, group)
        return pltpu.make_async_remote_copy(
            src_ref=src, dst_ref=dst, send_sem=swap_send.at[i], recv_sem=swap_recv.at[i],
            device_id=partner, device_id_type=MESH,
        )

    def local(i):
        src, dst = swaps[i]
        return pltpu.make_async_copy(src, dst, swap_recv.at[i])

    def fetch(*items):
        @pl.when(moves)
        def _():
            for i in items:
                remote(i).start()

        @pl.when(stays)
        def _():
            for i in items:
                local(i).start()

    def fetched(*items):
        @pl.when(moves)
        def _():
            for i in items:
                remote(i).wait()

        @pl.when(stays)
        def _():
            for i in items:
                local(i).wait()

    fetch(0, 1, 3, 2)
    keep_model = pltpu.make_async_copy(model_in, own_model, own_sem.at[0])
    keep_model.start()

    shape = (2 * nz, nz)
    distance = jnp.abs(
        lax.broadcasted_iota(jnp.int32, shape, 0) % nz - lax.broadcasted_iota(jnp.int32, shape, 1)
    )
    weights = jnp.zeros(shape, F32)
    for index, weight in enumerate(BAND):
        weights = jnp.where(distance == index + 1, weight, weights)
    band[...] = weights.astype(BF16)

    def clear_grad(i, carry):
        grad[i] = jnp.zeros((ny, nz), F32)
        return carry

    lax.fori_loop(0, rows, clear_grad, 0)

    fetched(0)

    spots_z = pack[STEPS + 1, 1:2, :]
    columns = lax.broadcasted_iota(jnp.int32, (nz, rec), 0).astype(F32) == spots_z

    def place(q, carry):
        for index, piece in enumerate(pieces(pack[q, 0:1, :])):
            targets[q, :, index * rec : (index + 1) * rec] = jnp.where(
                columns, piece.astype(F32), 0.0
            ).astype(BF16)
        return carry

    lax.fori_loop(0, STEPS + 1, place, 0)

    def spread(i, carry):
        line = lax.broadcasted_iota(jnp.int32, (ny, rec), 0) + (slab * rows + i) * ny
        hit = jnp.where(line.astype(F32) == pack[STEPS + 1, 0:1, :], 1.0, 0.0).astype(BF16)
        hits = jnp.concatenate([hit, hit, hit], axis=1)

        def amount(q):
            return lax.dot_general(
                hits, targets[q], (((1,), (1,)), ((), ())), preferred_element_type=F32
            )

        def one(q, carry):
            sources[q, i] = amount(q)
            return carry

        lax.fori_loop(0, STEPS, one, 0)
        counts[i] = amount(STEPS)
        return carry

    lax.fori_loop(0, rows, spread, 0)
    spot[...] = jnp.where(
        (lax.broadcasted_iota(jnp.int32, (ny, nz), 0).astype(F32) == pack[STEPS + 1, 3:4, 0:nz])
        & (lax.broadcasted_iota(jnp.int32, (ny, nz), 1).astype(F32) == pack[STEPS + 1, 4:5, 0:nz]),
        1.0,
        0.0,
    )

    def face(buf, field, u, side):
        slot = lax.rem(u, 2)
        src = jnp.where(side == 0, 4, rows)
        dst = jnp.where(side == 0, rows + 4, 0)
        return pltpu.make_async_remote_copy(
            src_ref=buf.at[slot, pl.ds(src, 4), pl.ds(8, ny), :],
            dst_ref=buf.at[slot, pl.ds(dst, 4), pl.ds(8, ny), :],
            send_sem=halo_send.at[field, u, side],
            recv_sem=halo_recv.at[field, u, 1 - side],
            device_id=toward(side),
            device_id_type=MESH,
        )

    def arrival(buf, field, u, side):
        slot = lax.rem(u, 2)
        dst = jnp.where(side == 0, 0, rows + 4)
        block = buf.at[slot, pl.ds(dst, 4), pl.ds(8, ny), :]
        return pltpu.make_async_remote_copy(
            src_ref=block, dst_ref=block,
            send_sem=halo_send.at[field, u, side],
            recv_sem=halo_recv.at[field, u, side],
            device_id=toward(side),
            device_id_type=MESH,
        )

    def layer(buf, field, u, j):
        slot = lax.rem(u, 2)
        src = jnp.where(far_side == 0, 4 + j, rows + 3 - j)
        dst = jnp.where(far_side == 0, rows + 4 + j, 3 - j)
        return pltpu.make_async_remote_copy(
            src_ref=buf.at[slot, src, pl.ds(8, ny), :],
            dst_ref=buf.at[slot, dst, pl.ds(8, ny), :],
            send_sem=far_send.at[field, u, j],
            recv_sem=far_recv.at[field, u, j],
            device_id=toward(far_side),
            device_id_type=MESH,
        )

    def layer_arrival(buf, field, u, j):
        slot = lax.rem(u, 2)
        dst = jnp.where(far_side == 0, 3 - j, rows + 4 + j)
        place = buf.at[slot, dst, pl.ds(8, ny), :]
        return pltpu.make_async_remote_copy(
            src_ref=place, dst_ref=place,
            send_sem=far_send.at[field, u, j],
            recv_sem=far_recv.at[field, u, j],
            device_id=toward(far_side),
            device_id_type=MESH,
        )

    def send_near(buf, field, u):
        @pl.when(has(near_side))
        def _():
            face(buf, field, u, near_side).start()

    def send_all(buf, field):
        @pl.when(has(far_side))
        def _():
            for j in range(4):
                layer(buf, field, 0, j).start()

        send_near(buf, field, 0)

    def laplace(buf, slot, i):
        field = buf[slot, 4 + i, 8 : 8 + ny, :]
        image = (3.0 * CENTRE) * field
        for index, weight in enumerate(COEFFS):
            k = index + 1
            image = image + weight * (
                (buf[slot, 4 + i + k, 8 : 8 + ny, :] + buf[slot, 4 + i - k, 8 : 8 + ny, :])
                + (buf[slot, 4 + i, 8 + k : 8 + k + ny, :] + buf[slot, 4 + i, 8 - k : 8 - k + ny, :])
            )
        high, middle, low = pieces(field)
        along = jnp.dot(
            jnp.concatenate([high, middle], axis=1), band[...], preferred_element_type=F32
        ) + jnp.dot(low, band[0:nz, :], preferred_element_type=F32)
        return field, image + along * BAND_SCALE

    def advance(buf, field, u, plane):
        slot = lax.rem(u, 2)

        def run(first, count):
            lax.fori_loop(first, first + count, lambda i, carry: (plane(u, slot, i), carry)[1], 0)

        run(4, rows - 8)

        @pl.when(has(near_side))
        def _():
            arrival(buf, field, u, near_side).wait_recv()

            @pl.when(u > 0)
            def _():
                face(buf, field, u - 1, near_side).wait_send()

        run(jnp.where(near_side == 0, 0, rows - 4), 4)

        @pl.when(u < STEPS - 1)
        def _():
            send_near(buf, field, u + 1)

        even = lax.rem(u, 2) == 0

        def one(n, carry):
            j = jnp.where(even, 3 - n, n)

            @pl.when(has(far_side))
            def _():
                @pl.when(even)
                def _():
                    layer_arrival(buf, field, u, n).wait_recv()

                @pl.when(jnp.logical_and(jnp.logical_not(even), n == 0))
                def _():
                    for m in (3, 2, 1, 0):
                        layer_arrival(buf, field, u, m).wait_recv()

                @pl.when(u > 0)
                def _():
                    layer(buf, field, u - 1, j).wait_send()

            plane(u, slot, jnp.where(far_side == 0, j, rows - 1 - j))

            @pl.when(jnp.logical_and(has(far_side), u < STEPS - 1))
            def _():
                layer(buf, field, u + 1, j).start()

            return carry

        lax.fori_loop(0, 4, one, 0)

    def settle(buf, field):
        @pl.when(has(near_side))
        def _():
            face(buf, field, STEPS - 1, near_side).wait_send()

        @pl.when(has(far_side))
        def _():
            for j in range(4):
                layer(buf, field, STEPS - 1, j).wait_send()

    def wave_plane(t, slot, i):
        now, image = laplace(wave, slot, i)
        position = (slab * rows + i).astype(F32)
        push = jnp.where(pack[STEPS + 1, 2:3, 0:nz] == position, pack[t, 1:2, 0:nz], 0.0)
        new = (
            2.0 * now - wave[1 - slot, 4 + i, 8 : 8 + ny, :] + model[i] * image + push * spot[...]
        )
        wave[1 - slot, 4 + i, 8 : 8 + ny, :] = new
        images[t, i] = image
        sources[t, i] = counts[i] * new - sources[t, i]

    def adjoint_plane(u, slot, i):
        t = STEPS - 1 - u
        now, image = laplace(adj, slot, i)
        new = 2.0 * now - adj[1 - slot, 4 + i, 8 : 8 + ny, :] + model[i] * image + sources[t, i]
        adj[1 - slot, 4 + i, 8 : 8 + ny, :] = new
        grad[i] = grad[i] + new * images[t, i]

    fetched(1)
    send_all(wave, 0)
    fetched(3)

    def model_part(o, index, peer):
        return pltpu.make_async_remote_copy(
            src_ref=block(model, index), dst_ref=block(model, index),
            send_sem=model_send.at[o - 1], recv_sem=model_recv.at[o - 1],
            device_id={"shot": 2 * peer + core, "dom": dom}, device_id_type=MESH,
        )

    @pl.when(moves)
    def _():
        for o in range(1, groups):
            model_part(o, group, lax.rem(group + o, groups)).start()

    fetched(2)
    fetch(4, 5)

    @pl.when(moves)
    def _():
        for o in range(1, groups):
            origin = lax.rem(group + groups - o, groups)
            model_part(o, origin, origin).wait_recv()
            model_part(o, group, lax.rem(group + o, groups)).wait_send()

    def forward(t, carry):
        @pl.when(t == STEPS - 1)
        def _():
            fetched(4, 5)
            send_all(adj, 1)

        advance(wave, 0, t, wave_plane)
        return carry

    lax.fori_loop(0, STEPS, forward, 0)
    settle(wave, 0)

    def backward(u, carry):
        advance(adj, 1, u, adjoint_plane)
        return carry

    lax.fori_loop(0, STEPS, backward, 0)
    settle(adj, 1)

    def part(ref, index, n):
        return ref.at[pl.ds(index * chunk + n * depth, depth)]

    def to_across(q, n):
        return pltpu.make_async_remote_copy(
            src_ref=part(grad, q, n), dst_ref=part(other, q, n),
            send_sem=sum_send.at[q, n], recv_sem=sum_recv.at[q, n],
            device_id=across, device_id_type=MESH,
        )

    def to_group(o, n):
        peer = lax.rem(group + o, groups)
        return pltpu.make_async_remote_copy(
            src_ref=part(grad, peer, n), dst_ref=part(parts.at[o - 1], 0, n),
            send_sem=part_send.at[o - 1, n], recv_sem=part_recv.at[o - 1, n],
            device_id={"shot": 2 * peer + core, "dom": dom}, device_id_type=MESH,
        )

    def share(o, n, index, peer):
        return pltpu.make_async_remote_copy(
            src_ref=part(total, index, n), dst_ref=part(total, index, n),
            send_sem=all_send.at[o - 1, n], recv_sem=all_recv.at[o - 1, n],
            device_id={"shot": 2 * peer + core, "dom": dom}, device_id_type=MESH,
        )

    def to_core(o, n):
        index = lax.rem(group + groups - o, groups)
        return pltpu.make_async_remote_copy(
            src_ref=part(total, index, n), dst_ref=part(total, index, n),
            send_sem=core_send.at[o, n], recv_sem=core_recv.at[o, n],
            device_id=beside, device_id_type=MESH,
        )

    def top(n):
        return pltpu.make_async_remote_copy(
            src_ref=tops.at[dom], dst_ref=tops.at[dom],
            send_sem=top_send.at[n], recv_sem=top_recv.at[dom],
            device_id=member(n), device_id_type=MESH,
        )

    def top_arrival(d):
        return pltpu.make_async_remote_copy(
            src_ref=tops.at[d], dst_ref=tops.at[d],
            send_sem=top_send.at[0], recv_sem=top_recv.at[d],
            device_id=beside, device_id_type=MESH,
        )

    keep_model.wait()

    @pl.when(moves)
    def _():
        for n in range(pieces_of):
            for o in list(range(1, groups)) + [0]:
                to_across(lax.rem(group + o, groups), n).start()
        for n in range(pieces_of):
            to_core(0, n).wait_recv()
        for o in range(1, groups):
            for n in range(pieces_of):
                to_core(o, n).wait_recv()
        for n in range(pieces_of):
            for o in range(groups):
                to_across(o, n).wait_send()

    @pl.when(stays)
    def _():
        for n in range(pieces_of + 1):
            if n < pieces_of:
                for o in range(1, groups):
                    index = lax.rem(group + o, groups)
                    to_across(index, n).wait_recv()
                    for m in range(n * depth, n * depth + depth):
                        i = index * chunk + m
                        grad[i] = grad[i] + other[i]
                    to_group(o, n).start()
            if n > 0:
                last = n - 1
                to_across(group, last).wait_recv()
                for o in range(1, groups):
                    to_group(o, last).wait_recv()
                for m in range(last * depth, last * depth + depth):
                    i = group * chunk + m
                    value = grad[i] + other[i]
                    for o in range(1, groups):
                        value = value + parts[o - 1, m]
                    total[i] = value
                for o in range(1, groups):
                    share(o, last, group, lax.rem(group + o, groups)).start()
                to_core(0, last).start()
        for o in range(1, groups):
            origin = lax.rem(group + groups - o, groups)
            for n in range(pieces_of):
                share(o, n, origin, origin).wait_recv()
                to_core(o, n).start()

        def largest(i, best):
            return jnp.maximum(best, jnp.max(jnp.abs(total[i]).reshape(ny // 8, 8, nz), axis=0))

        tops[dom] = lax.fori_loop(0, rows, largest, jnp.zeros((8, nz), F32))

        def tell(n, carry):
            @pl.when(n != me)
            def _():
                top(n).start()

            return carry

        lax.fori_loop(0, 2 * doms, tell, 0)

    def hear(d, carry):
        @pl.when(jnp.logical_or(d != dom, moves))
        def _():
            top_arrival(d).wait_recv()

        return carry

    lax.fori_loop(0, doms, hear, 0)
    best = lax.fori_loop(0, doms, lambda d, b: jnp.maximum(b, tops[d]), jnp.zeros((8, nz), F32))
    divisor = jnp.max(best, keepdims=True) + EPSILON

    def finish(i, carry):
        direction = total[i] / divisor
        direction_ref[i] = direction
        new_model_ref[i] = own_model[i] * (1.0 - STEP_FRACTION * direction)
        return carry

    lax.fori_loop(0, rows, finish, 0)

    @pl.when(stays)
    def _():
        def told(n, carry):
            @pl.when(n != me)
            def _():
                top(n).wait_send()

            return carry

        lax.fori_loop(0, 2 * doms, told, 0)
        for n in range(pieces_of):
            for o in range(1, groups):
                to_group(o, n).wait_send()
                share(o, n, group, lax.rem(group + o, groups)).wait_send()
            for o in range(groups):
                to_core(o, n).wait_send()


def packed(rows, ny, nz, wavelet, source_cell, receiver_cells, observed):
    rec = receiver_cells.shape[1]
    zeros = jnp.zeros((STEPS, rec), F32)
    steps = jnp.stack(
        [observed[0], jnp.broadcast_to(wavelet[0][:, None], (STEPS, rec))] + [zeros] * 6, axis=1
    )
    cell = jnp.broadcast_to(source_cell[0], (rec,))
    receivers = receiver_cells[0]
    ones = jnp.stack([jnp.ones((rec,), F32)] + [zeros[0]] * 7)
    places = [receivers // nz, receivers % nz, cell // (ny * nz), cell // nz % ny, cell % nz]
    places = jnp.stack([p.astype(F32) for p in places] + [zeros[0]] * 3)
    return jnp.concatenate([steps, ones[None], places[None]], axis=0)


def on_device(
    shots, doms, model_slab, wave_prev, wave_now, adjoint_next, adjoint_now,
    wavelet, source_cell, receiver_cells, observed,
):
    rows, ny, nz = model_slab.shape
    rec = receiver_cells.shape[1]
    groups = shots // 2
    pack = packed(rows, ny, nz, wavelet, source_cell, receiver_cells, observed)
    dma = pltpu.SemaphoreType.DMA
    padded = (2, rows + 8, ny + 16, nz)
    slab = (rows, ny, nz)
    pieces_of = math.gcd(4, rows // groups)
    return pl.pallas_call(
        functools.partial(kernel, shots, doms),
        out_shape=(jax.ShapeDtypeStruct(slab, F32),) * 2,
        in_specs=[pl.BlockSpec(memory_space=pl.ANY)] * 6,
        out_specs=(pl.BlockSpec(memory_space=pltpu.VMEM),) * 2,
        scratch_shapes=[
            pltpu.VMEM(padded, F32),
            pltpu.VMEM(padded, F32),
            pltpu.VMEM((STEPS,) + slab, F32),
            pltpu.VMEM((STEPS,) + slab, F32),
            pltpu.VMEM(slab, F32),
            pltpu.VMEM(slab, F32),
            pltpu.VMEM(slab, F32),
            pltpu.VMEM(pack.shape, F32),
            pltpu.VMEM((STEPS + 1, nz, 3 * rec), BF16),
            pltpu.VMEM((2 * nz, nz), BF16),
            pltpu.VMEM((ny, nz), F32),
            pltpu.VMEM(slab, F32),
            pltpu.VMEM((groups - 1, rows // groups, ny, nz), F32),
            pltpu.VMEM(slab, F32),
            pltpu.VMEM(slab, F32),
            pltpu.VMEM((doms, 8, nz), F32),
            dma((6,)),
            dma((6,)),
            dma((2, STEPS, 2)),
            dma((2, STEPS, 2)),
            dma((2, STEPS, 4)),
            dma((2, STEPS, 4)),
            dma((groups - 1,)),
            dma((groups - 1,)),
            dma((groups, pieces_of)),
            dma((groups, pieces_of)),
            dma((groups - 1, pieces_of)),
            dma((groups - 1, pieces_of)),
            dma((groups - 1, pieces_of)),
            dma((groups - 1, pieces_of)),
            dma((groups, pieces_of)),
            dma((groups, pieces_of)),
            dma((2 * doms,)),
            dma((doms,)),
            dma((1,)),
        ],
        compiler_params=pltpu.CompilerParams(
            collective_id=0, has_side_effects=True, vmem_limit_bytes=48 * 1024 * 1024
        ),
    )(pack, model_slab, wave_prev[0], wave_now[0], adjoint_next[0], adjoint_now[0])


def solution(mesh):
    placed = (
        P("dom", None, None),
        P("shot", "dom", None, None),
        P("shot", "dom", None, None),
        P("shot", "dom", None, None),
        P("shot", "dom", None, None),
        P("shot", None),
        P("shot"),
        P("shot", None),
        P("shot", None, None),
    )
    return jax.shard_map(
        functools.partial(on_device, mesh.shape["shot"], mesh.shape["dom"]),
        mesh=mesh,
        in_specs=placed,
        out_specs=(P("dom", None, None), P("dom", None, None)),
        check_vma=False,
    )
```

time: 575 us -> 153 us (0.27); the launches traced: 566 us -> 152 us
  waiting for transfers between devices: 156 us -> 0 us
  Pallas kernels: 0 us -> 142 us
  other arithmetic: 139 us -> 0.11 us
  local copies, waits for them, and re-layouts: 131 us -> 8.56 us
  starting transfers between devices: 96 us -> 0 us
  blocking collectives: 22 us -> 0 us
  between operations: 22.4 us -> 1.42 us
    pallas_call x0 -> x1, Pallas kernels: none -> 142 us  [on_device(): pl.pallas_call(functools.partial(kernel, shots, doms), out_shape=(jax.Sha...]
    ppermute x32 -> x0, waiting for transfers between devices: 114 us -> none  [the longest x16 88.4 us: padded_2(): lax.ppermute(head, axis, [((i + 1) % count, i) for i in range(ends)])]
    add x17 -> x0, other arithmetic: 101 us -> none  [the longest x8 51.9 us: on_device(): newer = 2.0 * current - older + model_slab * image]
    slice x146 -> x0, local copies, waits for them, and re-layouts: 97.6 us -> none  [the longest x128 88.1 us: shifted(): lax.slice_in_dim(field, offset, length, axis=axis)]
    ppermute x32 -> x0, starting transfers between devices: 96 us -> none  [the longest x16 72 us: padded_2(): lax.ppermute(tail, axis, [(i, (i + 1) % count) for i in range(ends)])]
    psum x1 -> x0, waiting for transfers between devices: 42 us -> none  [on_device(): total = lax.psum(gradient, 'shot')]
    scatter-add x16 -> x0, other arithmetic: 33.9 us -> none  [add_at(): return field.reshape(-1).at[slots].add(values).reshape(field.shape)]
    gather x8 -> x0, local copies, waits for them, and re-layouts: 29.9 us -> none  [on_device(): values = newer.reshape(-1)[receiver_slots] - observed[0, tick]]
  transfers between devices with their start and end apart: 33 -> 0, of which waited for: 25 -> 0; matrix products, arithmetic and copies ran while one was open for 13% -> 0% of each run, Pallas kernels for 0% -> 0%
where the time goes in v1:
time: 153 us; the launch traced here: 152 us
  Pallas kernels  142 us (93%)
  local copies, waits for them, and re-layouts  8.56 us (6%)
    pallas_call x1, Pallas kernels, on_device(): pl.pallas_call(functools.partial(kernel, shots, doms), out_shape=(jax.Sha...  142 us
    unnamed x16, local copies, waits for them, and re-layouts  8.21 us

profile of v1, /device:TPU:0, one launch (start us, length us, event | category | flops | bytes accessed | tf_op | source)
XLA Modules:
  0.0 152.4 jit_solution(2341727279841770857)
XLA Ops:
  1.4 0.0 copy-start.5
  1.4 0.7 copy-done.5
  2.0 0.0 copy-start.6
  2.1 0.6 copy-done.6
  2.7 0.1 reshape.8
  2.8 0.1 pad.1.clone
  2.9 0.1 pad.3.clone
  3.0 0.0 copy-start.4
  3.0 0.1 pad.2.clone
  3.0 0.6 copy-done.4
  3.7 0.0 copy-start.3
  3.7 0.7 copy-done.3
  4.4 0.1 pad_maximum_fusion.pack_in
  4.5 0.0 copy-start
  4.5 1.2 copy-done
  5.7 0.0 copy-start.1
  5.7 1.2 copy-done.1
  6.9 0.0 copy-start.2
  6.9 1.2 copy-done.2
  8.1 142.3 %shard_map.104 = (f32[16,128,128]{2,1,0:T(8,128)S(1)}, f32[16,128,128]{2,1,0:T(8,128)S(1)}) custom-call(f32[10,8,256]{2,1,0:T(8,128)S(1)} %pad_maximum_fusion.pack_in, f32[16,128,128]{2,1,0:T(8,128)S(1)} %copy-done, f32[16,128,128]{2,1,0:T(8,128)S(1)} %bitcast.11, f32[16,128,128]{2,1,0:T(8,128)S(1)} %bitcast.12, f32[16,128,128]{2,1,0:T(8,128)} %bitcast.13, ...), custom_call_target="tpu_custom_call" | custom-call | tf_op jit(solution)/shard_map/pallas_call | solution.py:586
  150.4 1.0 copy.14
  151.4 1.0 copy.15
  (10 shorter events, 0.1 us)
Async XLA Ops:
  1.4 0.7 copy-start.5
  2.0 0.7 copy-start.6
  3.0 0.7 copy-start.4
  3.7 0.7 copy-start.3
  4.5 1.2 copy-start
  5.7 1.2 copy-start.1
  6.9 1.2 copy-start.2

commit v2 on v1

--- a/solution.py
+++ b/solution.py
@@ -272,26 +272,30 @@
 
         send_near(buf, field, 0)
 
-    def laplace(buf, slot, i):
-        field = buf[slot, 4 + i, 8 : 8 + ny, :]
+    def laplace(buf, slot, i, n):
+        def at(x, y):
+            return buf[slot, pl.ds(4 + i + x, n), 8 + y : 8 + y + ny, :]
+
+        field = at(0, 0)
+        high, middle, low = pieces(field.reshape(n * ny, nz))
+        along = jnp.dot(
+            jnp.concatenate([high, middle], axis=1), band[...], preferred_element_type=F32
+        ) + jnp.dot(low, band[0:nz, :], preferred_element_type=F32)
         image = (3.0 * CENTRE) * field
         for index, weight in enumerate(COEFFS):
             k = index + 1
-            image = image + weight * (
-                (buf[slot, 4 + i + k, 8 : 8 + ny, :] + buf[slot, 4 + i - k, 8 : 8 + ny, :])
-                + (buf[slot, 4 + i, 8 + k : 8 + k + ny, :] + buf[slot, 4 + i, 8 - k : 8 - k + ny, :])
-            )
-        high, middle, low = pieces(field)
-        along = jnp.dot(
-            jnp.concatenate([high, middle], axis=1), band[...], preferred_element_type=F32
-        ) + jnp.dot(low, band[0:nz, :], preferred_element_type=F32)
-        return field, image + along * BAND_SCALE
+            image = image + weight * ((at(k, 0) + at(-k, 0)) + (at(0, k) + at(0, -k)))
+        return field, image + along.reshape(n, ny, nz) * BAND_SCALE
 
     def advance(buf, field, u, plane):
         slot = lax.rem(u, 2)
 
         def run(first, count):
-            lax.fori_loop(first, first + count, lambda i, carry: (plane(u, slot, i), carry)[1], 0)
+            def two(m, carry):
+                plane(u, slot, first + 2 * m, 2)
+                return carry
+
+            lax.fori_loop(0, count // 2, two, 0)
 
         run(4, rows - 8)
 
@@ -329,7 +333,7 @@
                 def _():
                     layer(buf, field, u - 1, j).wait_send()
 
-            plane(u, slot, jnp.where(far_side == 0, j, rows - 1 - j))
+            plane(u, slot, jnp.where(far_side == 0, j, rows - 1 - j), 1)
 
             @pl.when(jnp.logical_and(has(far_side), u < STEPS - 1))
             def _():
@@ -349,23 +353,31 @@
             for j in range(4):
                 layer(buf, field, STEPS - 1, j).wait_send()
 
-    def wave_plane(t, slot, i):
-        now, image = laplace(wave, slot, i)
-        position = (slab * rows + i).astype(F32)
+    def wave_plane(t, slot, i, n):
+        now, image = laplace(wave, slot, i, n)
+        here = pl.ds(i, n)
+        inner = pl.ds(4 + i, n)
+        position = (lax.broadcasted_iota(jnp.int32, (n, 1, nz), 0) + (slab * rows + i)).astype(F32)
         push = jnp.where(pack[STEPS + 1, 2:3, 0:nz] == position, pack[t, 1:2, 0:nz], 0.0)
         new = (
-            2.0 * now - wave[1 - slot, 4 + i, 8 : 8 + ny, :] + model[i] * image + push * spot[...]
-        )
-        wave[1 - slot, 4 + i, 8 : 8 + ny, :] = new
-        images[t, i] = image
-        sources[t, i] = counts[i] * new - sources[t, i]
-
-    def adjoint_plane(u, slot, i):
+            2.0 * now - wave[1 - slot, inner, 8 : 8 + ny, :] + model[here] * image + push * spot[...]
+        )
+        source = counts[here] * new - sources[t, here]
+        wave[1 - slot, inner, 8 : 8 + ny, :] = new
+        images[t, here] = image
+        sources[t, here] = source
+
+    def adjoint_plane(u, slot, i, n):
         t = STEPS - 1 - u
-        now, image = laplace(adj, slot, i)
-        new = 2.0 * now - adj[1 - slot, 4 + i, 8 : 8 + ny, :] + model[i] * image + sources[t, i]
-        adj[1 - slot, 4 + i, 8 : 8 + ny, :] = new
-        grad[i] = grad[i] + new * images[t, i]
+        now, image = laplace(adj, slot, i, n)
+        here = pl.ds(i, n)
+        inner = pl.ds(4 + i, n)
+        new = (
+            2.0 * now - adj[1 - slot, inner, 8 : 8 + ny, :] + model[here] * image + sources[t, here]
+        )
+        gradient = grad[here] + new * images[t, here]
+        adj[1 - slot, inner, 8 : 8 + ny, :] = new
+        grad[here] = gradient
 
     fetched(1)
     send_all(wave, 0)
@@ -626,7 +638,7 @@
             dma((1,)),
         ],
         compiler_params=pltpu.CompilerParams(
-            collective_id=0, has_side_effects=True, vmem_limit_bytes=48 * 1024 * 1024
+            collective_id=0, has_side_effects=True, vmem_limit_bytes=60 * 1024 * 1024
         ),
     )(pack, model_slab, wave_prev[0], wave_now[0], adjoint_next[0], adjoint_now[0])
 

time: 153 us -> 151 us (0.987)
  local copies, waits for them, and re-layouts: 8.56 us -> 6.3 us
    unnamed x16 -> x12, local copies, waits for them, and re-layouts: 8.21 us -> 5.96 us
where the time goes in v2:
time: 151 us
  Pallas kernels  143 us (95%)
  local copies, waits for them, and re-layouts  6.3 us (4%)
    pallas_call x1, Pallas kernels, on_device(): pl.pallas_call(functools.partial(kernel, shots, doms), out_shape=(jax.Sha...  143 us
    unnamed x12, local copies, waits for them, and re-layouts  5.96 us

profile of v2, /device:TPU:0, one launch (start us, length us, event | category | flops | bytes accessed | tf_op | source)
XLA Modules:
  0.0 151.2 jit_solution(17649596089862797832)
XLA Ops:
  1.4 0.0 copy-start.3
  1.4 0.7 copy-done.3
  2.0 0.0 copy-start.4
  2.1 0.6 copy-done.4
  2.7 0.1 reshape.8
  2.8 0.1 pad.1.clone
  2.9 0.1 pad.3.clone
  3.0 0.0 copy-start.2
  3.0 0.1 pad.2.clone
  3.0 0.6 copy-done.2
  3.7 0.0 copy-start.1
  3.7 0.7 copy-done.1
  4.4 0.7 pad_maximum_fusion.pack_in
  5.1 142.7 %shard_map.104 = (f32[16,128,128]{2,1,0:T(8,128)}, f32[16,128,128]{2,1,0:T(8,128)}) custom-call(f32[10,8,256]{2,1,0:T(8,128)} %pad_maximum_fusion.pack_in, f32[16,128,128]{2,1,0:T(8,128)} %model_in.1, f32[16,128,128]{2,1,0:T(8,128)} %bitcast.11, f32[16,128,128]{2,1,0:T(8,128)} %bitcast.12, f32[16,128,128]{2,1,0:T(8,128)} %bitcast.13, f32[16,128,128]{2,1,0:T(8,128)} %bitcast.14), custom_call_target="tpu_custom_call" | custom-call | tf_op jit(solution)/shard_map/pallas_call | solution.py:598
  147.8 0.0 copy-start
  147.9 2.4 %copy.14 = f32[16,128,128]{2,1,0:T(8,128)} copy(f32[16,128,128]{2,1,0:T(8,128)} %get-tuple-element.6) | data formatting | bytes 2097152
  150.2 0.0 copy-done
  150.2 1.0 copy.15
  (10 shorter events, 0.1 us)
Async XLA Ops:
  1.4 0.7 copy-start.3
  2.0 0.7 copy-start.4
  3.0 0.7 copy-start.2
  3.7 0.7 copy-start.1
  147.8 2.4 %copy-start = (f32[16,128,128]{2,1,0:T(8,128)S(1)}, f32[16,128,128]{2,1,0:T(8,128)}, u32[]{:S(2)}) copy-start(f32[16,128,128]{2,1,0:T(8,128)} %get-tuple-element.7) | copy-start | bytes 3145732
